TPU v7x, 32 devices: a whole 2x2x4 slice. The times are simulated.
32 devices in a mesh: row: 16 (over z, y, x), col: 2 (over core).
Axes of the slice: x: 2, y: 2, z: 4, core: 2. Of those that a mesh axis runs over, the one named last changes fastest.
Arguments:
- green_function: float32 [32, 32, 64, 128], P('row', 'col'), may hold values from -3 to 3
- hamiltonian: float32 [64, 128], replicated, may hold values from -3 to 3
Outputs:
- green_out: float32 [32, 32, 64, 128], P('row', 'col')
All inputs are finite; a program needn't handle non-finite values.
Results may differ from a plain program's by a relative error of at most 0.00019.
Values sent between devices are 32-bit elements; how exact they have to be, the bound alone decides.
A program may use at most 64 MiB of HBM per device.

v0:
```python
import jax
import jax.numpy as jnp
from jax import lax
from jax.sharding import PartitionSpec as P

STEPS = 2


time_step = 0.1


def rotate(values):
    half = values.shape[-1] // 2
    return jnp.concatenate([-values[..., half:], values[..., :half]], axis=-1)


def body(green_function, hamiltonian):
    local_rows = green_function.shape[0]
    local_cols = green_function.shape[1]
    orbits = green_function.shape[2]
    row_first = lax.axis_index("row") * local_rows
    col_first = lax.axis_index("col") * local_cols
    first = row_first + jnp.arange(local_rows, dtype=jnp.int32)[:, None]
    second = col_first + jnp.arange(local_cols, dtype=jnp.int32)[None, :]
    weight = jnp.where(
        second < first,
        jnp.float32(1.0),
        jnp.where(second == first, jnp.float32(0.5), jnp.float32(0.0)),
    )
    ham_real = hamiltonian[:, :orbits]
    ham_imag = hamiltonian[:, orbits:]
    for repeat in range(STEPS):
        real_part = green_function[..., :orbits]
        imag_part = green_function[..., orbits:]
        magnitude = real_part * real_part + imag_part * imag_part
        scaled = jnp.concatenate([magnitude, magnitude], axis=-1) * green_function
        sigma = -(time_step * weight)[:, :, None, None] * scaled
        sigma_pair = jnp.concatenate([-sigma, rotate(sigma)], axis=2)
        gathered = lax.all_gather(green_function, "row", axis=0, tiled=True)
        partial_value = jnp.einsum(
            "tsxq,uskq->tukx", sigma_pair, gathered, precision=lax.Precision.HIGHEST
        )
        owned = lax.psum_scatter(partial_value, "col", scatter_dimension=1, tiled=True)
        integral = (
            owned.reshape(local_rows, local_cols, orbits, 2, orbits)
            .transpose(0, 1, 4, 3, 2)
            .reshape(local_rows, local_cols, orbits, 2 * orbits)
        )
        driven = jnp.einsum(
            "ij,tujq->tuiq", ham_real, green_function, precision=lax.Precision.HIGHEST
        )
        driven = driven + jnp.einsum(
            "ij,tujq->tuiq", ham_imag, rotate(green_function), precision=lax.Precision.HIGHEST
        )
        driven = driven + integral
        green_function = green_function - time_step * rotate(driven)
    return green_function


def solution(mesh):
    in_specs = (P("row", "col", None, None), P())
    out_specs = P("row", "col", None, None)
    return jax.shard_map(body, mesh=mesh, in_specs=in_specs, out_specs=out_specs, check_vma=False)
```

profile of v0, /device:TPU:8, one launch (start us, length us, event | category | flops | bytes accessed | tf_op | source)
XLA Modules:
  0.0 487.4 jit_solution(18106789630151251516)
XLA Ops:
  6.5 0.7 all-gather.3.cloned.1.call-update
  7.4 0.3 copy-done.1
  7.8 1.7 slice_negate_fusion.5
  9.4 0.4 fusion.50
  9.9 1.4 slice_negate_fusion.3
  11.2 189.9 %all-gather.3.cloned.1.call-done = f32[32,16,64,128]{3,2,1,0:T(8,128)} async-done(((f32[2,16,64,128]{3,2,1,0:T(8,128)}), f32[32,16,64,128]{3,2,1,0:T(8,128)}) %all-gather.3.cloned.1.call-update) | async-done | bytes 16777232 | tf_op jit(solution)/shard_map/all_gather | solution.py:39
  201.1 17.4 %fusion.12 = f32[2,32,64,128]{3,2,1,0:T(8,128)S(1)} fusion(f32[32,16,64,128]{3,2,1,0:T(8,128)} %all-gather.3.cloned.1.call-done, f32[2,16,64,64]{3,2,1,0:T(8,128)} %get-tuple-element.22, f32[2,16,64,64]{3,2,1,0:T(8,128)S(1)} %get-tuple-element.21, f32[2,16,64,128]{3,2,1,0:T(8,128)S(1)} %get-tuple-element.7), kind=kOutput, calls=%fused_computation.15 | convolution fusion | flops 12885950464 | bytes 20971520 | tf_op jit(solution)/shard_map/tsxq,uskq->tukx/dot_general | solution.py:40
  218.7 2.5 copy.20
  221.5 0.5 copy-done.6
  222.0 2.1 fusion.36
  224.1 7.3 %reduce-scatter.8.cloned.1.call-done = f32[16,16384]{1,0:T(8,128)} async-done(((f32[32,16384]{1,0:T(8,128)}), f32[16,16384]{1,0:T(8,128)}) %reduce-scatter.8.cloned.1.call-update) | async-done | bytes 1048592
  231.4 2.4 copy.18
  233.8 2.5 reshape.95
  236.3 3.6 copy.5
  239.9 3.5 reshape.82
  243.4 2.9 fusion.21
  246.3 0.4 slice_negate_fusion.2
  246.6 1.3 fusion.26
  248.3 0.9 copy-done
  249.2 1.7 slice_negate_fusion.4
  250.9 0.4 fusion.48
  251.3 1.4 slice_negate_fusion.1
  252.7 186.2 %all-gather.5.cloned.1.call-done = f32[32,16,64,128]{3,2,1,0:T(8,128)} async-done(((f32[2,16,64,128]{3,2,1,0:T(8,128)}), f32[32,16,64,128]{3,2,1,0:T(8,128)}) %all-gather.5.cloned.1.call-update) | async-done | bytes 16777232 | tf_op jit(solution)/shard_map/all_gather | solution.py:39
  438.8 17.7 %fusion.15 = f32[2,32,64,128]{3,2,0,1:T(8,128)} fusion(f32[2,16,64,64]{3,2,1,0:T(8,128)} %get-tuple-element.15, f32[2,16,64,64]{3,2,1,0:T(8,128)S(1)} %get-tuple-element.14, f32[2,16,64,128]{3,2,1,0:T(8,128)S(1)} %get-tuple-element.5, f32[32,16,64,128]{3,2,1,0:T(8,128)} %all-gather.5.cloned.1.call-done), kind=kOutput, calls=%fused_computation.16 | convolution fusion | flops 12885950464 | bytes 20971520 | tf_op jit(solution)/shard_map/tsxq,uskq->tukx/dot_general | solution.py:40
  456.6 2.1 fusion.34
  458.6 8.0 %reduce-scatter.6.cloned.1.call-done = f32[2,16,64,128]{3,2,0,1:T(8,128)} async-done(((f32[2,32,64,128]{3,2,0,1:T(8,128)}), f32[2,16,64,128]{3,2,0,1:T(8,128)}) %reduce-scatter.6.cloned.1.call-update) | async-done | bytes 1048592 | tf_op jit(solution)/shard_map/reduce_scatter | solution.py:43
  466.6 2.5 reshape.83
  469.1 3.6 copy.6
  472.8 3.5 reshape.84
  476.2 2.9 fusion.19
  479.1 0.4 slice_negate_fusion
  479.5 1.3 fusion.31
  (22 shorter events, 0.8 us)
Async XLA Ops:
  6.5 1.2 copy-start.1
  6.5 194.6 %all-gather.3.cloned.1.call-start = ((), (), s32[]{:S(2)}) async-start(), calls=%async_computation.2 | async-start | bytes 17825792 | tf_op jit(solution)/shard_map/all_gather | solution.py:39
  7.3 224.1 %reduce-scatter.8.cloned.1.call-start = ((), (), s32[]{:S(2)}) async-start(), calls=%async_computation.5 | async-start | bytes 3145728
  221.2 0.8 copy-start.6
  221.3 217.5 %all-gather.5.cloned.1.call-start = ((), (), s32[]{:S(2)}) async-start(), calls=%async_computation.3 | async-start | bytes 17825792 | tf_op jit(solution)/shard_map/all_gather | solution.py:39
  239.9 3.5 copy-start.2
  239.9 3.5 copy-start.3
  248.0 1.2 copy-start
  248.0 218.6 %reduce-scatter.6.cloned.1.call-start = ((), (), s32[]{:S(2)}) async-start(), calls=%async_computation.4 | async-start | bytes 3145728 | tf_op jit(solution)/shard_map/reduce_scatter | solution.py:43
  472.8 3.5 copy-start.4
  472.8 3.5 copy-start.5
Sparse Core Ops, SparseCore 0:
  10.1 190.9 all-gather.2
  221.4 9.9 reduce-scatter.7
  248.1 190.6 all-gather.4
  456.7 9.9 reduce-scatter.5
where the time goes:
time: 489 us; the launch traced here: 487 us
  waiting for transfers between devices  392 us (80%)
  matrix products  45 us (9%)
  local copies, waits for them, and re-layouts  26.1 us (5%)
  between operations  13.2 us (3%)
  other arithmetic  10.4 us (2%)
    all_gather x2, waiting for transfers between devices, body(): gathered = lax.all_gather(green_function, 'row', axis=0, tiled=True)  376 us
    dot_general x2, matrix products, body(): jnp.einsum('tsxq,uskq->tukx', sigma_pair, gathered, precision=lax.Precisi...  35.2 us
    reshape x4, local copies, waits for them, and re-layouts, body(): owned.reshape(local_rows, local_cols, orbits, 2, orbits)  12.2 us
  transfers between devices with their start and end apart: 4, of which 4 were waited for; matrix products, arithmetic and copies ran while one was open for 2% of the time, Pallas kernels for 0%

commit v1 on v0

v1 whole, which is shorter than its diff:
```python
import functools

import jax
import jax.numpy as jnp
from jax import lax
from jax.experimental import pallas as pl
from jax.experimental.pallas import tpu as pltpu
from jax.sharding import PartitionSpec as P

STEPS = 2
time_step = 0.1

GROUP = 4
CHUNK = 4
MESH = pl.DeviceIdType.MESH
NT = (((1,), (1,)), ((), ()))
NN = (((1,), (0,)), ((), ()))


def dot(a, b, dims):
    return lax.dot_general(a, b, dims, preferred_element_type=jnp.float32)


def split(x):
    hi = x.astype(jnp.bfloat16)
    lo = (x - hi.astype(jnp.float32)).astype(jnp.bfloat16)
    return hi, lo


def kernel(
    planes, cols, green, ham, out, held, plane, res, red_t, red_u,
    acc_t, acc_u, hat_hi, hat_lo, sig_hi, sig_lo, sx, hx_hi, hx_lo, h_acc,
    z_send, z_recv, x_send, y_send, f_send, p_recv,
    rt_send, rt_recv, ru_send, ru_recv, t_send, t_recv, u_send, u_recv,
):
    lr, lc, orb, wide = green.shape
    half = wide // 2
    B, A, C = GROUP, planes, cols
    pu = B * lr
    ppc = lc // pu
    ch = min(CHUNK, lc)
    nj = lc // ch
    kw = ch * wide

    row = lax.axis_index("row")
    col = lax.axis_index("col")
    z, p = row // B, row % B
    xn = p + 1 - 2 * (p % 2)
    yn = (p + 2) % B
    dn = (xn + 2) % B
    s_first = col * lc
    cz = z // ppc

    def dev(zz, pp, cc):
        return (zz * B + pp, cc)

    def remote(src, dst, ss, rs, to):
        return pltpu.make_async_remote_copy(
            src_ref=src, dst_ref=dst, send_sem=ss, recv_sem=rs, device_id=to, device_id_type=MESH
        )

    bar = pltpu.get_barrier_semaphore()
    for q in (xn, yn, dn):
        pl.semaphore_signal(bar, inc=1, device_id=dev(z, q, col), device_id_type=MESH)
    for k in range(1, A):
        pl.semaphore_signal(bar, inc=1, device_id=dev((z + k) % A, p, col), device_id_type=MESH)
    for k in range(1, C):
        pl.semaphore_signal(bar, inc=1, device_id=dev(z, p, (col + k) % C), device_id_type=MESH)

    lane = lax.broadcasted_iota(jnp.int32, (orb, wide), 1)
    sign = jnp.where(lane < half, jnp.float32(-1.0), jnp.float32(1.0))

    def rot(x):
        return pltpu.roll(x, half, 1) * sign

    def copy_in(i, _):
        h, m = i // lc, i % lc
        held[0, z, h, m] = green[h, m]
        return 0

    lax.fori_loop(0, lr * lc, copy_in, 0)
    pl.semaphore_wait(bar, (B - 1) + (A - 1) + (C - 1))

    ham_hi, ham_lo = split(ham[...])

    def needed(v, j):
        return s_first + j * ch <= (v * B + p) * lr + lr - 1

    def reached(j):
        return s_first + j * ch <= z * pu + pu - 1

    def hats(src, hi_ref, lo_ref, first):
        def one(i, _):
            h, m = i // lc, i % lc
            g = src[h, m]
            r0 = pl.multiple_of((first + h) * 2 * orb, 2 * orb)
            c0 = pl.multiple_of(m * wide, wide)
            hi, lo = split(g)
            hi_ref[pl.ds(r0, orb), pl.ds(c0, wide)] = hi
            lo_ref[pl.ds(r0, orb), pl.ds(c0, wide)] = lo
            hi, lo = split(rot(g))
            r1 = pl.multiple_of(r0 + orb, orb)
            hi_ref[pl.ds(r1, orb), pl.ds(c0, wide)] = hi
            lo_ref[pl.ds(r1, orb), pl.ds(c0, wide)] = lo
            return 0

        lax.fori_loop(0, lr * lc, one, 0)

    def sigma(g, t, m):
        s = s_first + m
        weight = jnp.where(s < t, jnp.float32(time_step), jnp.where(s == t, jnp.float32(0.5 * time_step), jnp.float32(0.0)))
        sq = g * g
        return split(weight * ((sq + pltpu.roll(sq, half, 1)) * g))

    def sigma_plane(src, q):
        def chunk(j, _):
            @pl.when(reached(j))
            def _():
                def one(i, _):
                    h, m = i // ch, j * ch + i % ch
                    hi, lo = sigma(src[h, m], (z * B + q) * lr + h, m)
                    r0 = pl.multiple_of((q * lr + h) * orb, orb)
                    c0 = pl.multiple_of(m * wide, wide)
                    sig_hi[pl.ds(r0, orb), pl.ds(c0, wide)] = hi
                    sig_lo[pl.ds(r0, orb), pl.ds(c0, wide)] = lo
                    return 0

                lax.fori_loop(0, lr * ch, one, 0)
            return 0

        lax.fori_loop(0, nj, chunk, 0)

    def step_body(step, _):
        own = held.at[step, z]

        def z_copy(v, j):
            part = held.at[step, v, :, pl.ds(j * ch, ch)]
            return remote(part, part, z_send.at[step, v, j], z_recv.at[step, v, j], dev((z + A - 1) % A, p, col))

        def each_chunk(v, action):
            def one(j, _):
                @pl.when(needed(v, j))
                def _():
                    action(v, j)
                return 0

            lax.fori_loop(0, nj, one, 0)

        def to_x(h):
            return remote(own.at[h], plane.at[step, p, h], x_send.at[step, h], p_recv.at[step, p, h], dev(z, xn, col))

        def to_y(h):
            return remote(own.at[h], plane.at[step, p, h], y_send.at[step, h], p_recv.at[step, p, h], dev(z, yn, col))

        def onward(h):
            src, to = (xn, yn) if h % 2 == 0 else (yn, xn)
            part = plane.at[step, src, h]
            return remote(part, part, f_send.at[step, h], p_recv.at[step, src, h], dev(z, to, col))

        def arrived(q, h):
            part = plane.at[step, q, h]
            remote(part, part, f_send.at[step, h], p_recv.at[step, q, h], dev(z, xn, col)).wait_recv()

        @pl.when(z > 0)
        def _():
            each_chunk(z, lambda v, j: z_copy(v, j).start())

        for h in range(lr):
            to_x(h).start()
            to_y(h).start()

        hats(own, hat_hi, hat_lo, p * lr)
        sigma_plane(own, p)
        for h in range(lr):
            r0 = pl.multiple_of((p * lr + h) * 2 * orb, 2 * orb)
            g_hi = hat_hi[pl.ds(r0, 2 * orb), :]
            g_lo = hat_lo[pl.ds(r0, 2 * orb), :]
            h_acc[pl.ds(h * orb, orb), :] = dot(ham_hi, g_hi, NN) + (dot(ham_hi, g_lo, NN) + dot(ham_lo, g_hi, NN))

        for h in range(lr):
            arrived(xn if h % 2 == 0 else yn, h)
            onward(h).start()

        def relay(v, j):
            z_copy(v, j).wait_recv()

            @pl.when(z > 0)
            def _():
                z_copy(v, j).start()

        @pl.when(z > 0)
        def _():
            @pl.when(z + 1 < A)
            def _():
                each_chunk(z + 1, relay)

        for h in range(lr):
            arrived(yn if h % 2 == 0 else xn, h)
        for q in (xn, yn):
            hats(plane.at[step, q], hat_hi, hat_lo, q * lr)
            sigma_plane(plane.at[step, q], q)

        @pl.when(z > 0)
        def _():
            def more(v, _):
                each_chunk(v, relay)
                return 0

            lax.fori_loop(z + 2, A, more, 0)

        for h in range(lr):
            arrived(dn, h)
        hats(plane.at[step, dn], hat_hi, hat_lo, dn * lr)
        sigma_plane(plane.at[step, dn], dn)

        def t_red(v, to):
            return remote(acc_t.at[v], red_t.at[step, v], rt_send.at[v], rt_recv.at[step, v], dev(z, p, to))

        def u_red(v, to):
            return remote(acc_u.at[v], red_u.at[step, v], ru_send.at[v], ru_recv.at[step, v], dev(z, p, to))

        def t_res(v):
            return remote(acc_t.at[v], res.at[step, z], t_send.at[v], t_recv.at[step, z], dev(v, p, col))

        def u_part(v, q, at):
            return (
                acc_u.at[v, pl.ds(pl.multiple_of(q * lr * orb, lr * orb), lr * orb), :],
                res.at[step, v, :, pl.ds(pl.multiple_of(at * lr * wide, lr * wide), lr * wide)],
            )

        def u_res(v, q):
            src, dst = u_part(v, q, p)
            return remote(src, dst, u_send.at[v, q], u_recv.at[step, v, p], dev(z, q, col))

        def place(owner):
            return (col + C - owner) % C

        down = (col + C - 1) % C

        def rows_v(v, _):
            @pl.when(v > z)
            def _():
                @pl.when(z == 0)
                def _():
                    each_chunk(v, lambda v, j: z_copy(v, j).wait_recv())

            acc_t[v] = jnp.zeros(acc_t.shape[1:], jnp.float32)

            def t_chunk(j, _):
                @pl.when(needed(v, j))
                def _():
                    def one(i, _):
                        h, m = i // ch, j * ch + i % ch
                        hi, lo = sigma(held[step, v, h, m], (v * B + p) * lr + h, m)
                        r0 = pl.multiple_of(h * orb, orb)
                        c0 = pl.multiple_of(m * wide, wide)
                        sx[pl.ds(r0, orb), pl.ds(c0, wide)] = hi
                        sx[pl.ds(pl.multiple_of(lr * orb + r0, orb), orb), pl.ds(c0, wide)] = lo
                        return 0

                    lax.fori_loop(0, lr * ch, one, 0)
                    ks = pl.ds(pl.multiple_of(j * kw, kw), kw)
                    both = dot(sx[:, ks], hat_hi[:, ks], NT)
                    low = dot(sx[pl.ds(0, lr * orb), ks], hat_lo[:, ks], NT)
                    acc_t[v] += both[: lr * orb] + (both[lr * orb :] + low)
                return 0

            lax.fori_loop(0, nj, t_chunk, 0)
            k = place(cz)
            if C > 1:
                @pl.when(k < C - 1)
                def _():
                    t_red(v, down).wait_recv()
                    acc_t[v] += red_t[step, v]

                @pl.when(k > 0)
                def _():
                    t_red(v, down).start()

            @pl.when(k == 0)
            def _():
                @pl.when(v > z)
                def _():
                    t_res(v).start()

                @pl.when(v == z)
                def _():
                    res[step, z] = acc_t[z]

            @pl.when(v > z)
            def _():
                hats(held.at[step, v], hx_hi, hx_lo, 0)
                acc_u[v] = jnp.zeros(acc_u.shape[1:], jnp.float32)

                def u_chunk(j, _):
                    @pl.when(reached(j))
                    def _():
                        ks = pl.ds(pl.multiple_of(j * kw, kw), kw)
                        hi, lo = sig_hi[:, ks], sig_lo[:, ks]
                        ghi, glo = hx_hi[:, ks], hx_lo[:, ks]
                        acc_u[v] += dot(hi, ghi, NT) + (dot(hi, glo, NT) + dot(lo, ghi, NT))
                    return 0

                lax.fori_loop(0, nj, u_chunk, 0)
                k = place(v // ppc)
                if C > 1:
                    @pl.when(k < C - 1)
                    def _():
                        u_red(v, down).wait_recv()
                        acc_u[v] += red_u[step, v]

                    @pl.when(k > 0)
                    def _():
                        u_red(v, down).start()

                @pl.when(k == 0)
                def _():
                    for q in (xn, yn, dn):
                        u_res(v, q).start()
                    src, dst = u_part(v, p, p)
                    dst[...] = src[...]
            return 0

        lax.fori_loop(z, A, rows_v, 0)

        def collect(i, _):
            w = col * ppc + i

            @pl.when(w < z)
            def _():
                part = res.at[step, w]
                remote(part, part, t_send.at[w], t_recv.at[step, w], dev(z, xn, col)).wait_recv()

            @pl.when(w > z)
            def _():
                for q in (xn, yn, dn):
                    part = res.at[step, w, :, pl.ds(pl.multiple_of(q * lr * wide, lr * wide), lr * wide)]
                    remote(part, part, u_send.at[w, q], u_recv.at[step, w, q], dev(z, xn, col)).wait_recv()

            def update(i, _):
                h, m = i // pu, i % pu
                u = (w - col * ppc) * pu + m
                r0 = pl.multiple_of(h * orb, orb)
                driven = h_acc[pl.ds(r0, orb), pl.ds(pl.multiple_of(u * wide, wide), wide)]
                driven = driven + res[step, w, pl.ds(r0, orb), pl.ds(pl.multiple_of(m * wide, wide), wide)]
                new = held[step, z, h, u] - time_step * rot(driven)

                @pl.when(step < STEPS - 1)
                def _():
                    held[step + 1, z, h, u] = new

                @pl.when(step == STEPS - 1)
                def _():
                    out[h, u] = new
                return 0

            lax.fori_loop(0, lr * pu, update, 0)
            return 0

        lax.fori_loop(0, ppc, collect, 0)

        for h in range(lr):
            to_x(h).wait_send()
            to_y(h).wait_send()
            onward(h).wait_send()

        def sent(v, _):
            @pl.when(z > 0)
            def _():
                each_chunk(v, lambda v, j: z_copy(v, j).wait_send())

            k = place(cz)

            @pl.when(k > 0)
            def _():
                t_red(v, down).wait_send()

            @pl.when(v > z)
            def _():
                @pl.when(k == 0)
                def _():
                    t_res(v).wait_send()

                ku = place(v // ppc)

                @pl.when(ku > 0)
                def _():
                    u_red(v, down).wait_send()

                @pl.when(ku == 0)
                def _():
                    for q in (xn, yn, dn):
                        u_res(v, q).wait_send()
            return 0

        lax.fori_loop(z, A, sent, 0)
        return 0

    lax.fori_loop(0, STEPS, step_body, 0)


def solution(mesh):
    rows, cols = mesh.shape["row"], mesh.shape["col"]
    planes = rows // GROUP

    def step(green, ham):
        lr, lc, orb, wide = green.shape
        pu = GROUP * lr
        nj = lc // min(CHUNK, lc)
        f32, bf16 = jnp.float32, jnp.bfloat16
        dma = pltpu.SemaphoreType.DMA
        big = (lr * orb, pu * wide)
        tall = (pu * orb, lr * wide)
        return pl.pallas_call(
            functools.partial(kernel, planes, cols),
            out_shape=jax.ShapeDtypeStruct(green.shape, f32),
            in_specs=[pl.BlockSpec(memory_space=pltpu.VMEM)] * 2,
            out_specs=pl.BlockSpec(memory_space=pltpu.VMEM),
            scratch_shapes=[
                pltpu.VMEM((STEPS, planes) + green.shape, f32),
                pltpu.VMEM((STEPS, GROUP) + green.shape, f32),
                pltpu.VMEM((STEPS, planes) + big, f32),
                pltpu.VMEM((STEPS, planes) + big, f32),
                pltpu.VMEM((STEPS, planes) + tall, f32),
                pltpu.VMEM((planes,) + big, f32),
                pltpu.VMEM((planes,) + tall, f32),
                pltpu.VMEM((pu * wide, lc * wide), bf16),
                pltpu.VMEM((pu * wide, lc * wide), bf16),
                pltpu.VMEM((pu * orb, lc * wide), bf16),
                pltpu.VMEM((pu * orb, lc * wide), bf16),
                pltpu.VMEM((2 * lr * orb, lc * wide), bf16),
                pltpu.VMEM((lr * wide, lc * wide), bf16),
                pltpu.VMEM((lr * wide, lc * wide), bf16),
                pltpu.VMEM((lr * orb, lc * wide), f32),
                dma((STEPS, planes, nj)), dma((STEPS, planes, nj)),
                dma((STEPS, lr)), dma((STEPS, lr)), dma((STEPS, lr)),
                dma((STEPS, GROUP, lr)),
                dma((planes,)), dma((STEPS, planes)),
                dma((planes,)), dma((STEPS, planes)),
                dma((planes,)), dma((STEPS, planes)),
                dma((planes, GROUP)), dma((STEPS, planes, GROUP)),
            ],
            compiler_params=pltpu.CompilerParams(
                collective_id=0, has_side_effects=True, vmem_limit_bytes=62 * 1024 * 1024
            ),
        )(green, ham)

    spec = P("row", "col", None, None)
    return jax.shard_map(step, mesh=mesh, in_specs=(spec, P()), out_specs=spec, check_vma=False)
```

time: 489 us -> 178 us (0.36)
  the two profiles are of different devices: /device:TPU:8 before, /device:TPU:9 now
where the time goes in v1:
time: 178 us
  Pallas kernels  176 us (99%)
  local copies, waits for them, and re-layouts  2.31 us (1%)
    pallas_call x1, Pallas kernels, step(): pl.pallas_call(functools.partial(kernel, planes, cols), out_shape=jax.Sha...  176 us

profile of v1, /device:TPU:9, one launch (start us, length us, event | category | flops | bytes accessed | tf_op | source)
XLA Modules:
  0.0 177.9 jit_solution(3686878903919080408)
XLA Ops:
  0.0 175.6 %shard_map.28 = f32[2,16,64,128]{3,2,1,0:T(8,128)} custom-call(f32[2,16,64,128]{3,2,1,0:T(8,128)} %green.1, f32[64,128]{1,0:T(8,128)} %ham.1), custom_call_target="tpu_custom_call" | custom-call | tf_op jit(solution)/shard_map/pallas_call | solution.py:414
  175.6 2.3 %copy.4 = f32[2,16,64,128]{3,2,1,0:T(8,128)} copy(f32[2,16,64,128]{3,2,1,0:T(8,128)} %shard_map.28) | data formatting | bytes 2097152

commit v2 on v1

--- a/solution.py
+++ b/solution.py
@@ -11,6 +11,7 @@
 time_step = 0.1
 
 GROUP = 4
+UNROLL = 8
 CHUNK = 4
 MESH = pl.DeviceIdType.MESH
 NT = (((1,), (1,)), ((), ()))
@@ -78,7 +79,7 @@
         held[0, z, h, m] = green[h, m]
         return 0
 
-    lax.fori_loop(0, lr * lc, copy_in, 0)
+    lax.fori_loop(0, lr * lc, copy_in, 0, unroll=UNROLL)
     pl.semaphore_wait(bar, (B - 1) + (A - 1) + (C - 1))
 
     ham_hi, ham_lo = split(ham[...])
@@ -104,7 +105,7 @@
             lo_ref[pl.ds(r1, orb), pl.ds(c0, wide)] = lo
             return 0
 
-        lax.fori_loop(0, lr * lc, one, 0)
+        lax.fori_loop(0, lr * lc, one, 0, unroll=UNROLL)
 
     def sigma(g, t, m):
         s = s_first + m
@@ -125,7 +126,7 @@
                     sig_lo[pl.ds(r0, orb), pl.ds(c0, wide)] = lo
                     return 0
 
-                lax.fori_loop(0, lr * ch, one, 0)
+                lax.fori_loop(0, lr * ch, one, 0, unroll=UNROLL)
             return 0
 
         lax.fori_loop(0, nj, chunk, 0)
@@ -258,7 +259,7 @@
                         sx[pl.ds(pl.multiple_of(lr * orb + r0, orb), orb), pl.ds(c0, wide)] = lo
                         return 0
 
-                    lax.fori_loop(0, lr * ch, one, 0)
+                    lax.fori_loop(0, lr * ch, one, 0, unroll=UNROLL)
                     ks = pl.ds(pl.multiple_of(j * kw, kw), kw)
                     both = dot(sx[:, ks], hat_hi[:, ks], NT)
                     low = dot(sx[pl.ds(0, lr * orb), ks], hat_lo[:, ks], NT)
@@ -354,7 +355,7 @@
                     out[h, u] = new
                 return 0
 
-            lax.fori_loop(0, lr * pu, update, 0)
+            lax.fori_loop(0, lr * pu, update, 0, unroll=UNROLL)
             return 0
 
         lax.fori_loop(0, ppc, collect, 0)

time: 178 us -> 165 us (0.927)
  the two profiles are of different devices: /device:TPU:9 before, /device:TPU:1 now
where the time goes in v2:
time: 165 us
  Pallas kernels  163 us (99%)
  local copies, waits for them, and re-layouts  2.31 us (1%)
    pallas_call x1, Pallas kernels, step(): pl.pallas_call(functools.partial(kernel, planes, cols), out_shape=jax.Sha...  163 us

profile of v2, /device:TPU:1, one launch (start us, length us, event | category | flops | bytes accessed | tf_op | source)
XLA Modules:
  0.0 165.0 jit_solution(3351163906926728585)
XLA Ops:
  0.0 162.7 %shard_map.28 = f32[2,16,64,128]{3,2,1,0:T(8,128)} custom-call(f32[2,16,64,128]{3,2,1,0:T(8,128)} %green.1, f32[64,128]{1,0:T(8,128)} %ham.1), custom_call_target="tpu_custom_call" | custom-call | tf_op jit(solution)/shard_map/pallas_call | solution.py:415
  162.7 2.3 %copy.4 = f32[2,16,64,128]{3,2,1,0:T(8,128)} copy(f32[2,16,64,128]{3,2,1,0:T(8,128)} %shard_map.28) | data formatting | bytes 2097152

commit v3 on v2

--- a/solution.py
+++ b/solution.py
@@ -170,159 +170,233 @@
             to_x(h).start()
             to_y(h).start()
 
+        def cols_of(j):
+            return pl.ds(pl.multiple_of(j * kw, kw), kw)
+
+        def build(v, j):
+            def one(i, _):
+                h, m = i // ch, j * ch + i % ch
+                hi, lo = sigma(held[step, v, h, m], (v * B + p) * lr + h, m)
+                r0 = pl.multiple_of(h * orb, orb)
+                c0 = pl.multiple_of(m * wide, wide)
+                sx[v, pl.ds(r0, orb), pl.ds(c0, wide)] = hi
+                sx[v, pl.ds(pl.multiple_of(lr * orb + r0, orb), orb), pl.ds(c0, wide)] = lo
+                return 0
+
+            lax.fori_loop(0, lr * ch, one, 0, unroll=UNROLL)
+
+        def t_dot(v, j, q=None):
+            ks = cols_of(j)
+            us = pl.ds(0, pu * wide) if q is None else pl.ds(pl.multiple_of(q * lr * wide, lr * wide), lr * wide)
+            both = dot(sx[v, :, ks], hat_hi[us, ks], NT)
+            low = dot(sx[v, pl.ds(0, lr * orb), ks], hat_lo[us, ks], NT)
+            acc_t[v, :, us] += both[: lr * orb] + (both[lr * orb :] + low)
+
+        def t_rows(v, *qs):
+            def one(v, j):
+                for q in qs:
+                    t_dot(v, j, q)
+
+            each_chunk(v, one)
+
+        def u_dot(v, j):
+            @pl.when(reached(j))
+            def _():
+                def one(i, _):
+                    h, m = i // ch, j * ch + i % ch
+                    g = held[step, v, h, m]
+                    r0 = pl.multiple_of(h * 2 * orb, 2 * orb)
+                    r1 = pl.multiple_of(r0 + orb, orb)
+                    c0 = pl.multiple_of((i % ch) * wide, wide)
+                    hi, lo = split(g)
+                    hx_hi[pl.ds(r0, orb), pl.ds(c0, wide)] = hi
+                    hx_lo[pl.ds(r0, orb), pl.ds(c0, wide)] = lo
+                    hi, lo = split(rot(g))
+                    hx_hi[pl.ds(r1, orb), pl.ds(c0, wide)] = hi
+                    hx_lo[pl.ds(r1, orb), pl.ds(c0, wide)] = lo
+                    return 0
+
+                lax.fori_loop(0, lr * ch, one, 0, unroll=UNROLL)
+                ks = cols_of(j)
+                hi, lo = sig_hi[:, ks], sig_lo[:, ks]
+                ghi, glo = hx_hi[...], hx_lo[...]
+                acc_u[v] += dot(hi, ghi, NT) + (dot(hi, glo, NT) + dot(lo, ghi, NT))
+
+        def t_red(v, to):
+            return remote(acc_t.at[v], red_t.at[step, v], rt_send.at[v], rt_recv.at[step, v], dev(z, p, to))
+
+        def u_red(v, to):
+            return remote(acc_u.at[v], red_u.at[step, v], ru_send.at[v], ru_recv.at[step, v], dev(z, p, to))
+
+        def t_res(v):
+            return remote(acc_t.at[v], res.at[step, z], t_send.at[v], t_recv.at[step, z], dev(v, p, col))
+
+        def u_part(v, q, at):
+            return (
+                acc_u.at[v, pl.ds(pl.multiple_of(q * lr * orb, lr * orb), lr * orb), :],
+                res.at[step, v, :, pl.ds(pl.multiple_of(at * lr * wide, lr * wide), lr * wide)],
+            )
+
+        def u_res(v, q):
+            src, dst = u_part(v, q, p)
+            return remote(src, dst, u_send.at[v, q], u_recv.at[step, v, p], dev(z, q, col))
+
+        def place(owner):
+            return (col + C - owner) % C
+
+        down = (col + C - 1) % C
+
+        def t_finish(v):
+            k = place(cz)
+            if C > 1:
+                @pl.when(k > 0)
+                def _():
+                    if C > 2:
+                        @pl.when(k < C - 1)
+                        def _():
+                            t_red(v, down).wait_recv()
+                            acc_t[v] += red_t[step, v]
+
+                    t_red(v, down).start()
+
+            @pl.when(k == 0)
+            def _():
+                if C > 1:
+                    t_red(v, down).wait_recv()
+
+                @pl.when(v > z)
+                def _():
+                    if C > 1:
+                        acc_t[v] += red_t[step, v]
+                    t_res(v).start()
+
+                @pl.when(v == z)
+                def _():
+                    if C > 1:
+                        res[step, z] = acc_t[z] + red_t[step, z]
+                    else:
+                        res[step, z] = acc_t[z]
+
+        def u_finish(v):
+            k = place(v // ppc)
+            if C > 1:
+                @pl.when(k < C - 1)
+                def _():
+                    u_red(v, down).wait_recv()
+                    acc_u[v] += red_u[step, v]
+
+                @pl.when(k > 0)
+                def _():
+                    u_red(v, down).start()
+
+            @pl.when(k == 0)
+            def _():
+                for q in (xn, yn, dn):
+                    u_res(v, q).start()
+                src, dst = u_part(v, p, p)
+                dst[...] = src[...]
+
+        def take(v, j):
+            z_copy(v, j).wait_recv()
+
+            @pl.when(z > 0)
+            def _():
+                z_copy(v, j).start()
+
         hats(own, hat_hi, hat_lo, p * lr)
         sigma_plane(own, p)
+
+        def clear(v, _):
+            acc_t[v] = jnp.zeros(acc_t.shape[1:], jnp.float32)
+            acc_u[v] = jnp.zeros(acc_u.shape[1:], jnp.float32)
+            return 0
+
+        lax.fori_loop(z, A, clear, 0)
+        each_chunk(z, build)
         for h in range(lr):
             r0 = pl.multiple_of((p * lr + h) * 2 * orb, 2 * orb)
             g_hi = hat_hi[pl.ds(r0, 2 * orb), :]
             g_lo = hat_lo[pl.ds(r0, 2 * orb), :]
             h_acc[pl.ds(h * orb, orb), :] = dot(ham_hi, g_hi, NN) + (dot(ham_hi, g_lo, NN) + dot(ham_lo, g_hi, NN))
+        t_rows(z, p)
 
         for h in range(lr):
             arrived(xn if h % 2 == 0 else yn, h)
             onward(h).start()
 
-        def relay(v, j):
-            z_copy(v, j).wait_recv()
-
-            @pl.when(z > 0)
-            def _():
-                z_copy(v, j).start()
-
-        @pl.when(z > 0)
+        @pl.when(z + 1 < A)
         def _():
-            @pl.when(z + 1 < A)
-            def _():
-                each_chunk(z + 1, relay)
+            each_chunk(z + 1, take)
+            each_chunk(z + 1, build)
+            t_rows(z + 1, p)
 
         for h in range(lr):
             arrived(yn if h % 2 == 0 else xn, h)
         for q in (xn, yn):
             hats(plane.at[step, q], hat_hi, hat_lo, q * lr)
             sigma_plane(plane.at[step, q], q)
-
-        @pl.when(z > 0)
+        t_rows(z, xn, yn)
+
+        @pl.when(z + 1 < A)
         def _():
-            def more(v, _):
-                each_chunk(v, relay)
-                return 0
-
-            lax.fori_loop(z + 2, A, more, 0)
+            t_rows(z + 1, xn, yn)
+
+        early = nj // 2
+
+        @pl.when(z + 2 < A)
+        def _():
+            def one(v, j):
+                @pl.when((z == 0) | (j < early))
+                def _():
+                    take(v, j)
+
+                @pl.when(z == 0)
+                def _():
+                    build(v, j)
+                    for q in (p, xn, yn):
+                        t_dot(v, j, q)
+
+            each_chunk(z + 2, one)
 
         for h in range(lr):
             arrived(dn, h)
         hats(plane.at[step, dn], hat_hi, hat_lo, dn * lr)
         sigma_plane(plane.at[step, dn], dn)
 
-        def t_red(v, to):
-            return remote(acc_t.at[v], red_t.at[step, v], rt_send.at[v], rt_recv.at[step, v], dev(z, p, to))
-
-        def u_red(v, to):
-            return remote(acc_u.at[v], red_u.at[step, v], ru_send.at[v], ru_recv.at[step, v], dev(z, p, to))
-
-        def t_res(v):
-            return remote(acc_t.at[v], res.at[step, z], t_send.at[v], t_recv.at[step, z], dev(v, p, col))
-
-        def u_part(v, q, at):
-            return (
-                acc_u.at[v, pl.ds(pl.multiple_of(q * lr * orb, lr * orb), lr * orb), :],
-                res.at[step, v, :, pl.ds(pl.multiple_of(at * lr * wide, lr * wide), lr * wide)],
-            )
-
-        def u_res(v, q):
-            src, dst = u_part(v, q, p)
-            return remote(src, dst, u_send.at[v, q], u_recv.at[step, v, p], dev(z, q, col))
-
-        def place(owner):
-            return (col + C - owner) % C
-
-        down = (col + C - 1) % C
-
-        def rows_v(v, _):
-            @pl.when(v > z)
-            def _():
-                @pl.when(z == 0)
-                def _():
-                    each_chunk(v, lambda v, j: z_copy(v, j).wait_recv())
-
-            acc_t[v] = jnp.zeros(acc_t.shape[1:], jnp.float32)
-
-            def t_chunk(j, _):
-                @pl.when(needed(v, j))
-                def _():
-                    def one(i, _):
-                        h, m = i // ch, j * ch + i % ch
-                        hi, lo = sigma(held[step, v, h, m], (v * B + p) * lr + h, m)
-                        r0 = pl.multiple_of(h * orb, orb)
-                        c0 = pl.multiple_of(m * wide, wide)
-                        sx[pl.ds(r0, orb), pl.ds(c0, wide)] = hi
-                        sx[pl.ds(pl.multiple_of(lr * orb + r0, orb), orb), pl.ds(c0, wide)] = lo
-                        return 0
-
-                    lax.fori_loop(0, lr * ch, one, 0, unroll=UNROLL)
-                    ks = pl.ds(pl.multiple_of(j * kw, kw), kw)
-                    both = dot(sx[:, ks], hat_hi[:, ks], NT)
-                    low = dot(sx[pl.ds(0, lr * orb), ks], hat_lo[:, ks], NT)
-                    acc_t[v] += both[: lr * orb] + (both[lr * orb :] + low)
-                return 0
-
-            lax.fori_loop(0, nj, t_chunk, 0)
-            k = place(cz)
-            if C > 1:
-                @pl.when(k < C - 1)
-                def _():
-                    t_red(v, down).wait_recv()
-                    acc_t[v] += red_t[step, v]
-
-                @pl.when(k > 0)
-                def _():
-                    t_red(v, down).start()
-
-            @pl.when(k == 0)
-            def _():
-                @pl.when(v > z)
-                def _():
-                    t_res(v).start()
-
-                @pl.when(v == z)
-                def _():
-                    res[step, z] = acc_t[z]
-
-            @pl.when(v > z)
-            def _():
-                hats(held.at[step, v], hx_hi, hx_lo, 0)
-                acc_u[v] = jnp.zeros(acc_u.shape[1:], jnp.float32)
-
-                def u_chunk(j, _):
-                    @pl.when(reached(j))
+        t_rows(z, dn)
+        t_finish(z)
+
+        @pl.when(z + 1 < A)
+        def _():
+            t_rows(z + 1, dn)
+            t_finish(z + 1)
+            each_chunk(z + 1, u_dot)
+            u_finish(z + 1)
+
+        def late(v, _):
+            done = (z == 0) & (v == z + 2)
+
+            def one(v, j):
+                @pl.when(done)
+                def _():
+                    t_dot(v, j, dn)
+
+                @pl.when(jnp.logical_not(done))
+                def _():
+                    @pl.when((v > z + 2) | (j >= early))
                     def _():
-                        ks = pl.ds(pl.multiple_of(j * kw, kw), kw)
-                        hi, lo = sig_hi[:, ks], sig_lo[:, ks]
-                        ghi, glo = hx_hi[:, ks], hx_lo[:, ks]
-                        acc_u[v] += dot(hi, ghi, NT) + (dot(hi, glo, NT) + dot(lo, ghi, NT))
-                    return 0
-
-                lax.fori_loop(0, nj, u_chunk, 0)
-                k = place(v // ppc)
-                if C > 1:
-                    @pl.when(k < C - 1)
-                    def _():
-                        u_red(v, down).wait_recv()
-                        acc_u[v] += red_u[step, v]
-
-                    @pl.when(k > 0)
-                    def _():
-                        u_red(v, down).start()
-
-                @pl.when(k == 0)
-                def _():
-                    for q in (xn, yn, dn):
-                        u_res(v, q).start()
-                    src, dst = u_part(v, p, p)
-                    dst[...] = src[...]
+                        take(v, j)
+                    build(v, j)
+                    t_dot(v, j)
+
+                u_dot(v, j)
+
+            each_chunk(v, one)
+            t_finish(v)
+            u_finish(v)
             return 0
 
-        lax.fori_loop(z, A, rows_v, 0)
+        lax.fori_loop(z + 2, A, late, 0)
 
         def collect(i, _):
             w = col * ppc + i
@@ -429,9 +503,9 @@
                 pltpu.VMEM((pu * wide, lc * wide), bf16),
                 pltpu.VMEM((pu * orb, lc * wide), bf16),
                 pltpu.VMEM((pu * orb, lc * wide), bf16),
-                pltpu.VMEM((2 * lr * orb, lc * wide), bf16),
-                pltpu.VMEM((lr * wide, lc * wide), bf16),
-                pltpu.VMEM((lr * wide, lc * wide), bf16),
+                pltpu.VMEM((planes, 2 * lr * orb, lc * wide), bf16),
+                pltpu.VMEM((lr * wide, min(CHUNK, lc) * wide), bf16),
+                pltpu.VMEM((lr * wide, min(CHUNK, lc) * wide), bf16),
                 pltpu.VMEM((lr * orb, lc * wide), f32),
                 dma((STEPS, planes, nj)), dma((STEPS, planes, nj)),
                 dma((STEPS, lr)), dma((STEPS, lr)), dma((STEPS, lr)),

time: 165 us -> 146 us (0.88)
  Pallas kernels: 163 us -> 143 us
    pallas_call x1, Pallas kernels: 163 us -> 143 us  [step(): pl.pallas_call(functools.partial(kernel, planes, cols), out_shape=jax.Sha...]
where the time goes in v3:
time: 146 us
  Pallas kernels  143 us (98%)
  local copies, waits for them, and re-layouts  2.31 us (2%)
    pallas_call x1, Pallas kernels, step(): pl.pallas_call(functools.partial(kernel, planes, cols), out_shape=jax.Sha...  143 us

profile of v3, /device:TPU:1, one launch (start us, length us, event | category | flops | bytes accessed | tf_op | source)
XLA Modules:
  0.0 145.5 jit_solution(3083327477416147560)
XLA Ops:
  0.0 143.2 %shard_map.28 = f32[2,16,64,128]{3,2,1,0:T(8,128)} custom-call(f32[2,16,64,128]{3,2,1,0:T(8,128)} %green.1, f32[64,128]{1,0:T(8,128)} %ham.1), custom_call_target="tpu_custom_call" | custom-call | tf_op jit(solution)/shard_map/pallas_call | solution.py:489
  143.2 2.3 %copy.4 = f32[2,16,64,128]{3,2,1,0:T(8,128)} copy(f32[2,16,64,128]{3,2,1,0:T(8,128)} %shard_map.28) | data formatting | bytes 2097152

commit v4 on v3

--- a/solution.py
+++ b/solution.py
@@ -90,6 +90,9 @@
     def reached(j):
         return s_first + j * ch <= z * pu + pu - 1
 
+    def lowered(j):
+        return (z > 1) | ((z == 1) & (s_first + j * ch <= pu - 1))
+
     def hats(src, hi_ref, lo_ref, first):
         def one(i, _):
             h, m = i // lc, i % lc
@@ -162,9 +165,27 @@
             part = plane.at[step, q, h]
             remote(part, part, f_send.at[step, h], p_recv.at[step, q, h], dev(z, xn, col)).wait_recv()
 
-        @pl.when(z > 0)
-        def _():
-            each_chunk(z, lambda v, j: z_copy(v, j).start())
+        def z_down(v, j):
+            @pl.when(lowered(j))
+            def _():
+                z_copy(v, j).start()
+
+        def up_copy(j):
+            part = held.at[step, 0, :, pl.ds(j * ch, ch)]
+            return remote(part, part, z_send.at[step, 0, j], z_recv.at[step, 0, j], dev((z + 1) % A, p, col))
+
+        def each(action):
+            def one(j, _):
+                action(j)
+                return 0
+
+            lax.fori_loop(0, nj, one, 0)
+
+        each_chunk(z, z_down)
+        if A > 1:
+            @pl.when(z == 0)
+            def _():
+                each(lambda j: up_copy(j).start())
 
         for h in range(lr):
             to_x(h).start()
@@ -298,10 +319,14 @@
 
         def take(v, j):
             z_copy(v, j).wait_recv()
-
-            @pl.when(z > 0)
-            def _():
-                z_copy(v, j).start()
+            z_down(v, j)
+
+        def take_up(j):
+            up_copy(j).wait_recv()
+
+            @pl.when(z + 1 < A)
+            def _():
+                up_copy(j).start()
 
         hats(own, hat_hi, hat_lo, p * lr)
         sigma_plane(own, p)
@@ -312,6 +337,7 @@
             return 0
 
         lax.fori_loop(z, A, clear, 0)
+        acc_u[0] = jnp.zeros(acc_u.shape[1:], jnp.float32)
         each_chunk(z, build)
         for h in range(lr):
             r0 = pl.multiple_of((p * lr + h) * 2 * orb, 2 * orb)
@@ -324,9 +350,18 @@
             arrived(xn if h % 2 == 0 else yn, h)
             onward(h).start()
 
-        @pl.when(z + 1 < A)
+        above = (z > 0) & (z + 1 < A)
+
+        @pl.when(above)
         def _():
             each_chunk(z + 1, take)
+
+        @pl.when(z > 0)
+        def _():
+            each(take_up)
+
+        @pl.when(above)
+        def _():
             each_chunk(z + 1, build)
             t_rows(z + 1, p)
 
@@ -337,21 +372,18 @@
             sigma_plane(plane.at[step, q], q)
         t_rows(z, xn, yn)
 
-        @pl.when(z + 1 < A)
+        @pl.when(above)
         def _():
             t_rows(z + 1, xn, yn)
 
         early = nj // 2
 
-        @pl.when(z + 2 < A)
+        @pl.when((z > 0) & (z + 2 < A))
         def _():
             def one(v, j):
-                @pl.when((z == 0) | (j < early))
+                @pl.when(j < early)
                 def _():
                     take(v, j)
-
-                @pl.when(z == 0)
-                def _():
                     build(v, j)
                     for q in (p, xn, yn):
                         t_dot(v, j, q)
@@ -366,7 +398,7 @@
         t_rows(z, dn)
         t_finish(z)
 
-        @pl.when(z + 1 < A)
+        @pl.when(above)
         def _():
             t_rows(z + 1, dn)
             t_finish(z + 1)
@@ -374,18 +406,16 @@
             u_finish(z + 1)
 
         def late(v, _):
-            done = (z == 0) & (v == z + 2)
-
             def one(v, j):
+                done = (v == z + 2) & (j < early)
+
                 @pl.when(done)
                 def _():
                     t_dot(v, j, dn)
 
                 @pl.when(jnp.logical_not(done))
                 def _():
-                    @pl.when((v > z + 2) | (j >= early))
-                    def _():
-                        take(v, j)
+                    take(v, j)
                     build(v, j)
                     t_dot(v, j)
 
@@ -396,17 +426,38 @@
             u_finish(v)
             return 0
 
-        lax.fori_loop(z + 2, A, late, 0)
+        @pl.when(z > 0)
+        def _():
+            lax.fori_loop(z + 2, A, late, 0)
+            each(lambda j: u_dot(0, j))
+            u_finish(0)
+
+        @pl.when(z == 0)
+        def _():
+            def lowest(v, _):
+                def one(j):
+                    @pl.when(reached(j))
+                    def _():
+                        take(v, j)
+                        u_dot(v, j)
+
+                each(one)
+                u_finish(v)
+                return 0
+
+            lax.fori_loop(1, A, lowest, 0)
 
         def collect(i, _):
             w = col * ppc + i
 
-            @pl.when(w < z)
+            in_plane = (w > z) | ((w == 0) & (z > 0))
+
+            @pl.when((w < z) & (w > 0))
             def _():
                 part = res.at[step, w]
                 remote(part, part, t_send.at[w], t_recv.at[step, w], dev(z, xn, col)).wait_recv()
 
-            @pl.when(w > z)
+            @pl.when(in_plane)
             def _():
                 for q in (xn, yn, dn):
                     part = res.at[step, w, :, pl.ds(pl.multiple_of(q * lr * wide, lr * wide), lr * wide)]
@@ -439,34 +490,51 @@
             to_y(h).wait_send()
             onward(h).wait_send()
 
+        def u_sent(v):
+            ku = place(v // ppc)
+
+            @pl.when(ku > 0)
+            def _():
+                u_red(v, down).wait_send()
+
+            @pl.when(ku == 0)
+            def _():
+                for q in (xn, yn, dn):
+                    u_res(v, q).wait_send()
+
+        def left(v, j):
+            @pl.when(lowered(j))
+            def _():
+                z_copy(v, j).wait_send()
+
         def sent(v, _):
-            @pl.when(z > 0)
-            def _():
-                each_chunk(v, lambda v, j: z_copy(v, j).wait_send())
-
-            k = place(cz)
-
-            @pl.when(k > 0)
-            def _():
-                t_red(v, down).wait_send()
+            each_chunk(v, left)
+
+            @pl.when((v == z) | (z > 0))
+            def _():
+                k = place(cz)
+
+                @pl.when(k > 0)
+                def _():
+                    t_red(v, down).wait_send()
+
+                @pl.when((k == 0) & (v > z))
+                def _():
+                    t_res(v).wait_send()
 
             @pl.when(v > z)
             def _():
-                @pl.when(k == 0)
-                def _():
-                    t_res(v).wait_send()
-
-                ku = place(v // ppc)
-
-                @pl.when(ku > 0)
-                def _():
-                    u_red(v, down).wait_send()
-
-                @pl.when(ku == 0)
-                def _():
-                    for q in (xn, yn, dn):
-                        u_res(v, q).wait_send()
+                u_sent(v)
             return 0
+
+        @pl.when(z > 0)
+        def _():
+            u_sent(0)
+
+        if A > 1:
+            @pl.when(z + 1 < A)
+            def _():
+                each(lambda j: up_copy(j).wait_send())
 
         lax.fori_loop(z, A, sent, 0)
         return 0

time: 146 us -> 146 us (level)
  the two profiles are of different devices: /device:TPU:1 before, /device:TPU:8 now
where the time goes in v4:
time: 146 us; the launch traced here: 145 us
  Pallas kernels  143 us (98%)
  local copies, waits for them, and re-layouts  2.31 us (2%)
    pallas_call x1, Pallas kernels, step(): pl.pallas_call(functools.partial(kernel, planes, cols), out_shape=jax.Sha...  143 us

profile of v4, /device:TPU:8, one launch (start us, length us, event | category | flops | bytes accessed | tf_op | source)
XLA Modules:
  0.0 145.3 jit_solution(1312252716909306347)
XLA Ops:
  0.0 142.9 %shard_map.28 = f32[2,16,64,128]{3,2,1,0:T(8,128)} custom-call(f32[2,16,64,128]{3,2,1,0:T(8,128)} %green.1, f32[64,128]{1,0:T(8,128)} %ham.1), custom_call_target="tpu_custom_call" | custom-call | tf_op jit(solution)/shard_map/pallas_call | solution.py:557
  142.9 2.3 %copy.4 = f32[2,16,64,128]{3,2,1,0:T(8,128)} copy(f32[2,16,64,128]{3,2,1,0:T(8,128)} %shard_map.28) | data formatting | bytes 2097152

commit v5 on v4

--- a/solution.py
+++ b/solution.py
@@ -328,37 +328,48 @@
             def _():
                 up_copy(j).start()
 
-        hats(own, hat_hi, hat_lo, p * lr)
-        sigma_plane(own, p)
+        above = (z > 0) & (z + 1 < A)
+
+        def pass_on(j):
+            @pl.when(above)
+            def _():
+                take_up(j)
+
+                @pl.when(needed(z + 1, j))
+                def _():
+                    take(z + 1, j)
 
         def clear(v, _):
             acc_t[v] = jnp.zeros(acc_t.shape[1:], jnp.float32)
             acc_u[v] = jnp.zeros(acc_u.shape[1:], jnp.float32)
             return 0
 
-        lax.fori_loop(z, A, clear, 0)
-        acc_u[0] = jnp.zeros(acc_u.shape[1:], jnp.float32)
-        each_chunk(z, build)
-        for h in range(lr):
-            r0 = pl.multiple_of((p * lr + h) * 2 * orb, 2 * orb)
-            g_hi = hat_hi[pl.ds(r0, 2 * orb), :]
-            g_lo = hat_lo[pl.ds(r0, 2 * orb), :]
-            h_acc[pl.ds(h * orb, orb), :] = dot(ham_hi, g_hi, NN) + (dot(ham_hi, g_lo, NN) + dot(ham_lo, g_hi, NN))
-        t_rows(z, p)
-
-        for h in range(lr):
-            arrived(xn if h % 2 == 0 else yn, h)
-            onward(h).start()
-
-        above = (z > 0) & (z + 1 < A)
-
-        @pl.when(above)
-        def _():
-            each_chunk(z + 1, take)
-
-        @pl.when(z > 0)
-        def _():
-            each(take_up)
+        def prepare():
+            sigma_plane(own, p)
+            lax.fori_loop(z, A, clear, 0)
+            acc_u[0] = jnp.zeros(acc_u.shape[1:], jnp.float32)
+
+        def one_body():
+            each_chunk(z, build)
+            for h in range(lr):
+                r0 = pl.multiple_of((p * lr + h) * 2 * orb, 2 * orb)
+                g_hi = hat_hi[pl.ds(r0, 2 * orb), :]
+                g_lo = hat_lo[pl.ds(r0, 2 * orb), :]
+                h_acc[pl.ds(h * orb, orb), :] = dot(ham_hi, g_hi, NN) + (dot(ham_hi, g_lo, NN) + dot(ham_lo, g_hi, NN))
+            t_rows(z, p)
+
+        def neighbours():
+            for h in range(lr):
+                arrived(xn if h % 2 == 0 else yn, h)
+                onward(h).start()
+
+        hats(own, hat_hi, hat_lo, p * lr)
+        work = [prepare, one_body, neighbours]
+        for j in range(max(nj, len(work))):
+            if j < nj:
+                pass_on(j)
+            if j < len(work):
+                work[j]()
 
         @pl.when(above)
         def _():
@@ -429,6 +440,10 @@
         @pl.when(z > 0)
         def _():
             lax.fori_loop(z + 2, A, late, 0)
+            @pl.when(z + 1 == A)
+            def _():
+                each(take_up)
+
             each(lambda j: u_dot(0, j))
             u_finish(0)
 

time: 146 us -> 132 us (0.904)
  Pallas kernels: 143 us -> 130 us
    pallas_call x1, Pallas kernels: 143 us -> 130 us  [step(): pl.pallas_call(functools.partial(kernel, planes, cols), out_shape=jax.Sha...]
where the time goes in v5:
time: 132 us
  Pallas kernels  130 us (98%)
  local copies, waits for them, and re-layouts  2.31 us (2%)
    pallas_call x1, Pallas kernels, step(): pl.pallas_call(functools.partial(kernel, planes, cols), out_shape=jax.Sha...  130 us

profile of v5, /device:TPU:8, one launch (start us, length us, event | category | flops | bytes accessed | tf_op | source)
XLA Modules:
  0.0 132.3 jit_solution(1147671412484776606)
XLA Ops:
  0.0 130.0 %shard_map.28 = f32[2,16,64,128]{3,2,1,0:T(8,128)} custom-call(f32[2,16,64,128]{3,2,1,0:T(8,128)} %green.1, f32[64,128]{1,0:T(8,128)} %ham.1), custom_call_target="tpu_custom_call" | custom-call | tf_op jit(solution)/shard_map/pallas_call | solution.py:572
  130.0 2.3 %copy.4 = f32[2,16,64,128]{3,2,1,0:T(8,128)} copy(f32[2,16,64,128]{3,2,1,0:T(8,128)} %shard_map.28) | data formatting | bytes 2097152

commit v6 on v5

--- a/solution.py
+++ b/solution.py
@@ -181,11 +181,21 @@
 
             lax.fori_loop(0, nj, one, 0)
 
-        each_chunk(z, z_down)
-        if A > 1:
-            @pl.when(z == 0)
-            def _():
-                each(lambda j: up_copy(j).start())
+        def end_chunk(j, action):
+            @pl.when((z == A - 1) & lowered(j) & needed(z, j))
+            def _():
+                action(z_copy(z, j))
+
+            if A > 1:
+                @pl.when(z == 0)
+                def _():
+                    action(up_copy(j))
+
+        @pl.when(z < A - 1)
+        def _():
+            each_chunk(z, z_down)
+
+        end_chunk(0, lambda c: c.start())
 
         for h in range(lr):
             to_x(h).start()
@@ -331,6 +341,10 @@
         above = (z > 0) & (z + 1 < A)
 
         def pass_on(j):
+            end_chunk(j, lambda c: c.wait_send())
+            if j + 1 < nj:
+                end_chunk(j + 1, lambda c: c.start())
+
             @pl.when(above)
             def _():
                 take_up(j)
@@ -523,7 +537,9 @@
                 z_copy(v, j).wait_send()
 
         def sent(v, _):
-            each_chunk(v, left)
+            @pl.when((v > z) | (z < A - 1))
+            def _():
+                each_chunk(v, left)
 
             @pl.when((v == z) | (z > 0))
             def _():
@@ -547,7 +563,7 @@
             u_sent(0)
 
         if A > 1:
-            @pl.when(z + 1 < A)
+            @pl.when(above)
             def _():
                 each(lambda j: up_copy(j).wait_send())
 

time: 132 us -> 132 us (level)
  no operation moved by 1% of the time
where the time goes in v6:
time: 132 us
  Pallas kernels  130 us (98%)
  local copies, waits for them, and re-layouts  2.31 us (2%)
    pallas_call x1, Pallas kernels, step(): pl.pallas_call(functools.partial(kernel, planes, cols), out_shape=jax.Sha...  130 us

profile of v6, /device:TPU:8, one launch (start us, length us, event | category | flops | bytes accessed | tf_op | source)
XLA Modules:
  0.0 132.3 jit_solution(6106151509922242767)
XLA Ops:
  0.0 130.0 %shard_map.28 = f32[2,16,64,128]{3,2,1,0:T(8,128)} custom-call(f32[2,16,64,128]{3,2,1,0:T(8,128)} %green.1, f32[64,128]{1,0:T(8,128)} %ham.1), custom_call_target="tpu_custom_call" | custom-call | tf_op jit(solution)/shard_map/pallas_call | solution.py:588
  130.0 2.3 %copy.4 = f32[2,16,64,128]{3,2,1,0:T(8,128)} copy(f32[2,16,64,128]{3,2,1,0:T(8,128)} %shard_map.28) | data formatting | bytes 2097152

commit v7 on v6

--- a/solution.py
+++ b/solution.py
@@ -198,8 +198,7 @@
         end_chunk(0, lambda c: c.start())
 
         for h in range(lr):
-            to_x(h).start()
-            to_y(h).start()
+            (to_x(h) if h % 2 == 0 else to_y(h)).start()
 
         def cols_of(j):
             return pl.ds(pl.multiple_of(j * kw, kw), kw)
@@ -362,6 +361,8 @@
             sigma_plane(own, p)
             lax.fori_loop(z, A, clear, 0)
             acc_u[0] = jnp.zeros(acc_u.shape[1:], jnp.float32)
+            for h in range(lr):
+                (to_y(h) if h % 2 == 0 else to_x(h)).start()
 
         def one_body():
             each_chunk(z, build)
@@ -378,7 +379,7 @@
                 onward(h).start()
 
         hats(own, hat_hi, hat_lo, p * lr)
-        work = [prepare, one_body, neighbours]
+        work = [prepare, neighbours, one_body]
         for j in range(max(nj, len(work))):
             if j < nj:
                 pass_on(j)

time: 132 us -> 130 us (0.985)
  Pallas kernels: 130 us -> 128 us
    pallas_call x1, Pallas kernels: 130 us -> 128 us  [step(): pl.pallas_call(functools.partial(kernel, planes, cols), out_shape=jax.Sha...]
where the time goes in v7:
time: 130 us
  Pallas kernels  128 us (98%)
  local copies, waits for them, and re-layouts  2.31 us (2%)
    pallas_call x1, Pallas kernels, step(): pl.pallas_call(functools.partial(kernel, planes, cols), out_shape=jax.Sha...  128 us

profile of v7, /device:TPU:8, one launch (start us, length us, event | category | flops | bytes accessed | tf_op | source)
XLA Modules:
  0.0 130.1 jit_solution(5650111864232662394)
XLA Ops:
  0.0 127.8 %shard_map.28 = f32[2,16,64,128]{3,2,1,0:T(8,128)} custom-call(f32[2,16,64,128]{3,2,1,0:T(8,128)} %green.1, f32[64,128]{1,0:T(8,128)} %ham.1), custom_call_target="tpu_custom_call" | custom-call | tf_op jit(solution)/shard_map/pallas_call | solution.py:589
  127.8 2.3 %copy.4 = f32[2,16,64,128]{3,2,1,0:T(8,128)} copy(f32[2,16,64,128]{3,2,1,0:T(8,128)} %shard_map.28) | data formatting | bytes 2097152
